TPU v7x, 256 devices: a whole 4x4x8 slice. The times are simulated.
256 devices in a mesh: query: 32 (over x, z_hi, y), entity: 8 (over z_lo, core).
Axes of the slice: x: 4, y: 4, z: 8 (z_hi: 2, z_lo: 4; z = z_hi * 4 + z_lo), core: 2. Of those that a mesh axis runs over, the one named last changes fastest.
Arguments:
- anchor_ids: int32 [16384], P('query'), may hold values from 0 to 32767
- relation_ids: int32 [16384], P('query'), may hold values from 0 to 4130
- side_flags: int32 [16384], P('query'), may hold values from 0 to 1
- teacher_entities: bfloat16 [32768, 1000], P(('entity', 'query')), may hold values from -1.2 to 1.2, as said below
- student_entities: bfloat16 [32768, 128], P(('entity', 'query')), may hold values from -2.1 to 2.1, as said below
- teacher_relations: bfloat16 [4131, 1000], replicated, may hold values from -9 to 33, as said below
- student_relations: bfloat16 [4131, 128], replicated, may hold values from -9 to 63.6875, as said below
Outputs:
- divergence: float32 [16384], P('query')
- entity_grad: float32 [32768, 128], P(('entity', 'query'))
- query_grad: float32 [16384, 128], P('query')
Inputs may be any that keep to these rules, and one draw needn't show every extreme that they name: `teacher_entities`: Real-valued embeddings. `student_entities`: Real-valued embeddings. `teacher_relations`: Real-valued embeddings. `student_relations`: Real-valued embeddings.
All inputs are finite; a program needn't handle non-finite values.
Results may differ from a plain program's by a relative error of at most 0.013.
Values may be sent and summed in bfloat16 or wider, within the bound.
A program may use at most 128 MiB of HBM per device.

v0:
```python
import jax
import jax.numpy as jnp
from jax import lax
from jax.sharding import PartitionSpec as P


def query_vectors(anchor, relation, flags):
    half = anchor.shape[1] // 2
    sign = (2 * flags - 1).astype(jnp.float32)[:, None]
    a_re = anchor[:, :half]
    a_im = anchor[:, half:]
    r_re = relation[:, :half]
    r_im = relation[:, half:]
    real = a_re * r_re - sign * a_im * r_im
    imag = a_im * r_re + sign * a_re * r_im
    return jnp.concatenate([real, imag], axis=1).astype(jnp.bfloat16)


def per_device(
    anchor_ids,
    relation_ids,
    side_flags,
    teacher_entities,
    student_entities,
    teacher_relations,
    student_relations,
):
    teacher_slab, student_slab = (
        lax.all_gather(teacher_entities, "query", axis=0, tiled=True),
        lax.all_gather(student_entities, "query", axis=0, tiled=True),
    )
    slab = teacher_slab.shape[0]
    offset = lax.axis_index("entity") * slab
    local = anchor_ids - offset
    inside = ((local >= 0) & (local < slab))[:, None]
    safe = jnp.clip(local, 0, slab - 1)
    teacher_part = jnp.where(inside, jnp.take(teacher_slab, safe, axis=0).astype(jnp.float32), 0.0)
    student_part = jnp.where(inside, jnp.take(student_slab, safe, axis=0).astype(jnp.float32), 0.0)
    teacher_anchor, student_anchor = (
        lax.psum(teacher_part.astype(jnp.bfloat16), "entity").astype(jnp.float32),
        lax.psum(student_part.astype(jnp.bfloat16), "entity").astype(jnp.float32),
    )
    query_teacher = query_vectors(
        teacher_anchor,
        jnp.take(teacher_relations, relation_ids, axis=0).astype(jnp.float32),
        side_flags,
    )
    query_student = query_vectors(
        student_anchor,
        jnp.take(student_relations, relation_ids, axis=0).astype(jnp.float32),
        side_flags,
    )
    rows = query_teacher.shape[0]
    block = 1024
    count = slab // block
    teacher_blocks = teacher_slab.reshape(count, block, teacher_slab.shape[1])
    student_blocks = student_slab.reshape(count, block, student_slab.shape[1])

    def first_pass(carry, items):
        top_t, total_t, weighted, top_s, total_s = carry
        t = jnp.dot(query_teacher, items[0].T, preferred_element_type=jnp.float32)
        s = jnp.dot(query_student, items[1].T, preferred_element_type=jnp.float32)
        new_t = jnp.maximum(top_t, jnp.max(t, axis=1))
        factor_t = jnp.exp(top_t - new_t)
        expo_t = jnp.exp(t - new_t[:, None])
        total_t = total_t * factor_t + jnp.sum(expo_t, axis=1)
        weighted = weighted * factor_t + jnp.sum(expo_t * (t - s), axis=1)
        new_s = jnp.maximum(top_s, jnp.max(s, axis=1))
        total_s = total_s * jnp.exp(top_s - new_s) + jnp.sum(jnp.exp(s - new_s[:, None]), axis=1)
        kept = None
        return ((new_t, total_t, weighted, new_s, total_s), kept)

    lowest = jnp.full((rows,), -jnp.inf, jnp.float32)
    nothing = jnp.zeros((rows,), jnp.float32)
    stats, kept = lax.scan(
        first_pass, (lowest, nothing, nothing, lowest, nothing), (teacher_blocks, student_blocks)
    )
    top_t, total_t, weighted, top_s, total_s = stats
    best_t, best_s = lax.pmax((top_t, top_s), "entity")
    factor_t = jnp.exp(top_t - best_t)
    factor_s = jnp.exp(top_s - best_s)
    total_t, weighted, total_s = lax.psum(
        (total_t * factor_t, weighted * factor_t, total_s * factor_s), "entity"
    )
    top_t, top_s = (best_t, best_s)
    divergence = weighted / total_t - top_t - jnp.log(total_t) + top_s + jnp.log(total_s)

    def second_pass(q_grad, items):
        t = jnp.dot(query_teacher, items[0].T, preferred_element_type=jnp.float32)
        s = jnp.dot(query_student, items[1].T, preferred_element_type=jnp.float32)
        prob_t = jnp.exp(t - top_t[:, None]) / total_t[:, None]
        prob_s = jnp.exp(s - top_s[:, None]) / total_s[:, None]
        weights = (prob_s - prob_t).astype(jnp.bfloat16)
        grad_block = jnp.dot(weights.T, query_student, preferred_element_type=jnp.float32)
        q_grad = q_grad + jnp.dot(weights, items[1], preferred_element_type=jnp.float32)
        return (q_grad, grad_block)

    start = jnp.zeros((rows, query_student.shape[1]), jnp.float32)
    q_grad, grad_blocks = lax.scan(second_pass, start, (teacher_blocks, student_blocks))
    slab_grad = grad_blocks.reshape(slab, query_student.shape[1])
    entity_grad = lax.psum_scatter(slab_grad, "query", scatter_dimension=0, tiled=True)
    query_grad = lax.psum(q_grad, "entity")
    return (divergence, entity_grad, query_grad)


def solution(mesh):
    in_specs = (
        P("query"),
        P("query"),
        P("query"),
        P(("entity", "query"), None),
        P(("entity", "query"), None),
        P(),
        P(),
    )
    out_specs = (P("query"), P(("entity", "query"), None), P("query", None))
    return jax.shard_map(
        per_device, mesh=mesh, in_specs=in_specs, out_specs=out_specs, check_vma=False
    )
```

profile of v0, /device:TPU:32, one launch (start us, length us, event | category | flops | bytes accessed | tf_op | source)
XLA Modules:
  0.0 744.2 jit_solution(13715478936245018552)
XLA Ops:
  8.0 1.8 copy.10
  10.6 83.7 %all-gather.5.cloned.1.call-done = bf16[4096,128]{1,0:T(8,128)(2,1)} async-done(((bf16[128,128]{1,0:T(8,128)(2,1)}), bf16[4096,128]{1,0:T(8,128)(2,1)}) %all-gather.5.cloned.1.call-update) | async-done | bytes 1048592 | tf_op jit(solution)/shard_map/all_gather | solution.py:30
  94.3 2.4 gather_fusion.2
  96.7 0.9 select_convert_fusion.2
  97.5 149.9 %all-gather.3.cloned.1.call-done = bf16[4096,1000]{1,0:T(8,128)(2,1)} async-done(((bf16[128,1000]{1,0:T(8,128)(2,1)}), bf16[4096,1000]{1,0:T(8,128)(2,1)}) %all-gather.3.cloned.1.call-update) | async-done | bytes 8192016 | tf_op jit(solution)/shard_map/all_gather | solution.py:29
  247.4 7.2 gather_fusion
  254.6 1.3 select_convert_fusion
  256.1 12.1 %copy.11 = bf16[4131,1000]{1,0:T(8,128)(2,1)} copy(bf16[4131,1000]{0,1:T(8,128)(2,1)} %param.16) | data formatting | bytes 16524000 | tf_op args[5]
  268.3 8.0 %gather_fusion.1 = bf16[512,1000]{1,0:T(8,128)(2,1)} fusion(bf16[4131,1000]{1,0:T(8,128)(2,1)} %copy.11, s32[1024]{0:T(1024)S(1)} %pad_clamp_fusion), kind=kCustom, calls=%fused_computation.1 | custom fusion | bytes 2050048 | tf_op jit(solution)/shard_map/jit(_take)/gather | solution.py:45
  276.3 1.3 gather_fusion.3
  278.3 0.8 select_convert_fusion.3
  279.1 1.4 select_convert_fusion.1
  280.6 43.3 %all-reduce.8.cloned.1.call-done = (bf16[512,1000]{1,0:T(8,128)(2,1)}, bf16[512,128]{1,0:T(8,128)(2,1)}) async-done(((bf16[512,1000]{1,0:T(8,128)(2,1)}, bf16[512,128]{1,0:T(8,128)(2,1)}), (bf16[512,1000]{1,0:T(8,128)(2,1)}, bf16[512,128]{1,0:T(8,128)(2,1)})) %all-reduce.8.cloned.1.call-update) | async-done | bytes 1155088 | tf_op jit(solution)/shard_map/psum | solution.py:40
  323.9 1.5 convert_element_type.33
  325.4 1.0 subtract_convert_fusion.1
  326.4 1.3 pad_maximum_fusion
  328.1 46.0 %while.32 = (s32[]{:T(128)}, f32[512]{0:T(512)S(1)}, f32[512]{0:T(512)}, f32[512]{0:T(512)}, f32[512]{0:T(512)}, /*index=5*/f32[512]{0:T(512)}, bf16[4,1024,1000...) while((s32[]{:T(128)}, f32[512]{0:T(512)S(1)}, ...), condition=%wide.region_8.9_spmd.clone, body=%wide.region_2.8_spmd.clone.sunk | while | flops 1187518464 | bytes 12046677 | solution.py:75
  328.1 5.1 fusion.51
  333.2 2.0 fusion.52
  336.6 2.4 multiply_reduce_fusion.2
  339.6 5.1 fusion.51
  344.7 2.0 fusion.52
  348.1 2.4 multiply_reduce_fusion.2
  351.2 5.1 fusion.51
  356.2 2.0 fusion.52
  359.6 2.4 multiply_reduce_fusion.2
  362.7 5.1 fusion.51
  367.7 2.0 fusion.52
  371.1 2.4 multiply_reduce_fusion.2
  374.2 14.8 %all-reduce.1 = (f32[512]{0:T(512)}, f32[512]{0:T(512)}) all-reduce(f32[512]{0:T(512)} %get-tuple-element.120, f32[512]{0:T(512)S(1)} %get-tuple-element.118), channel_id=1, replica_groups=mesh['query'=32,'entity'=8] {'entity'}, use_global_device_ids=true, to_apply=%region_12.13 | all-reduce | flops 1024 | bytes 8192 | tf_op jit(solution)/shard_map/pmax | solution.py:79
  389.7 14.6 %all-reduce = (f32[512]{0:T(512)S(1)}, f32[512]{0:T(512)}, f32[512]{0:T(512)}) all-reduce(f32[512]{0:T(512)S(1)} %get-tuple-element.261, f32[512]{0:T(512)S(1)} %get-tuple-element.259, f32[512]{0:T(512)S(1)} %get-tuple-element.258), channel_id=1, replica_groups=mesh['query'=32,'entity'=8] {'entity'}, use_global_device_ids=true, to_apply=%region_13.14 | all-reduce | flops 1536 | bytes 12288 | tf_op jit(solution)/shard_map/psum | solution.py:82
  404.3 26.0 %while.33 = (s32[]{:T(128)}, f32[512,128]{1,0:T(8,128)S(1)}, f32[4,1024,128]{2,1,0:T(8,128)}, bf16[4,1024,128]{2,1,0:T(8,128)(2,1)}, bf16[512,128]{1,0:T(8,128)(...) while((s32[]{:T(128)}, f32[512,128]{1,0:T(8,128)S(1)}, ...), condition=%wide.region_15.16_spmd.clone, body=%wide.region_14.15_spmd.clone.sunk | while | flops 1454505984 | bytes 16531671 | solution.py:99
  404.3 3.2 fusion.62
  407.6 1.5 subtract_convert_fusion.4
  409.6 1.2 fusion.63
  410.8 3.2 fusion.62
  414.1 1.5 subtract_convert_fusion.4
  416.1 1.2 fusion.63
  417.3 3.2 fusion.62
  420.6 1.5 subtract_convert_fusion.4
  422.6 1.2 fusion.63
  423.8 3.2 fusion.62
  427.1 1.5 subtract_convert_fusion.4
  429.1 1.2 fusion.63
  431.6 1.3 log_add_fusion
  432.9 69.5 %all-reduce.6.cloned.1.call-done = f32[512,128]{1,0:T(8,128)} async-done(((f32[512,128]{1,0:T(8,128)}), f32[512,128]{1,0:T(8,128)}) %all-reduce.6.cloned.1.call-update) | async-done | bytes 262160 | tf_op jit(solution)/shard_map/psum | solution.py:102
  502.4 233.6 %reduce-scatter.2.cloned.1.call-done = f32[128,128]{1,0:T(8,128)} async-done(((f32[4096,128]{1,0:T(8,128)}), f32[128,128]{1,0:T(8,128)}) %reduce-scatter.2.cloned.1.call-update) | async-done | bytes 65552 | tf_op jit(solution)/shard_map/reduce_scatter | solution.py:101
  736.0 1.7 copy.43
  (141 shorter events, 14.7 us)
Async XLA Ops:
  7.2 269.1 %copy-start = (bf16[4131,128]{1,0:T(8,128)(2,1)S(1)}, bf16[4131,128]{1,0:T(8,128)(2,1)}, u32[]{:S(2)}) copy-start(bf16[4131,128]{1,0:T(8,128)(2,1)} %param.17) | copy-start | bytes 3172612
  7.2 87.1 %all-gather.5.cloned.1.call-start = ((), (), s32[]{:S(2)}) async-start(), calls=%async_computation.2 | async-start | bytes 1081344 | tf_op jit(solution)/shard_map/all_gather | solution.py:30
  7.9 239.5 %all-gather.3.cloned.1.call-start = ((), (), s32[]{:S(2)}) async-start(), calls=%async_computation.1 | async-start | bytes 8650752 | tf_op jit(solution)/shard_map/all_gather | solution.py:29
  9.8 314.0 %all-reduce.8.cloned.1.call-start = ((), (), s32[]{:S(2)}) async-start(), calls=%async_computation.5 | async-start | bytes 2359296 | tf_op jit(solution)/shard_map/psum | solution.py:40
  254.6 1.4 copy-start.13
  256.0 246.4 %all-reduce.6.cloned.1.call-start = ((), (), s32[]{:S(2)}) async-start(), calls=%async_computation.4 | async-start | bytes 524288 | tf_op jit(solution)/shard_map/psum | solution.py:102
  268.3 9.4 %copy-start.14 = (s32[512]{0:T(512)S(1)}, s32[512]{0:T(512)}, u32[]{:S(2)}) copy-start(s32[512]{0:T(512)} %param.13) | copy-start | bytes 6148
  323.9 1.5 copy-start.5
  323.9 1.5 copy-start.12
  326.4 1.3 copy-start.3
  336.5 2.4 copy-start.4
  336.5 2.4 copy-start.6
  336.5 2.4 copy-start.8
  336.6 2.4 copy-start.10
  339.0 0.6 copy-start.7
  339.0 0.6 copy-start.9
  339.0 0.6 copy-start.11
  348.1 2.4 copy-start.4
  348.1 2.4 copy-start.6
  348.1 2.4 copy-start.8
  348.1 2.4 copy-start.10
  350.5 0.6 copy-start.7
  350.5 0.6 copy-start.9
  350.5 0.6 copy-start.11
  359.6 2.4 copy-start.4
  359.6 2.4 copy-start.6
  359.6 2.4 copy-start.8
  359.6 2.4 copy-start.10
  362.0 0.6 copy-start.7
  362.0 0.6 copy-start.9
  371.1 2.4 copy-start.4
  371.1 2.4 copy-start.6
  371.1 2.4 copy-start.8
  371.1 2.4 copy-start.10
  373.5 0.6 copy-start.7
  373.5 0.6 copy-start.9
  404.3 3.2 copy-start.1
  404.3 3.2 copy-start.15
  410.8 3.2 copy-start.1
  410.8 3.2 copy-start.15
  417.3 3.2 copy-start.1
  417.3 3.2 copy-start.15
  423.8 3.2 copy-start.1
  423.8 3.2 copy-start.15
  430.3 0.7 copy-start.2
  430.3 1.3 copy-start.16
  430.3 1.3 copy-start.17
  431.0 305.0 %reduce-scatter.2.cloned.1.call-start = ((), (), s32[]{:S(2)}) async-start(), calls=%async_computation.3 | async-start | bytes 2162688 | tf_op jit(solution)/shard_map/reduce_scatter | solution.py:101
  (2 other events, 1.2 us)
Sparse Core Ops, SparseCore 0:
  11.4 82.7 all-gather.4
  98.4 149.0 all-gather.2
  256.1 67.6 all-reduce.7
  431.1 71.2 all-reduce.5
  505.5 230.4 reduce-scatter.1
where the time goes:
time: 745 us; the launch traced here: 744 us
  waiting for transfers between devices  581 us (78%)
  matrix products  53.9 us (7%)
  local copies, waits for them, and re-layouts  37.8 us (5%)
  blocking collectives  29.4 us (4%)
  other arithmetic  27 us (4%)
  between operations  14 us (2%)
    reduce_scatter x1, waiting for transfers between devices, per_device(): lax.psum_scatter(slab_grad, 'query', scatter_dimension=0, tiled=True)  234 us
    all_gather x1, waiting for transfers between devices, per_device(): lax.all_gather(teacher_entities, 'query', axis=0, tiled=True)  150 us
    all_gather x1, waiting for transfers between devices, per_device(): lax.all_gather(student_entities, 'query', axis=0, tiled=True)  83.7 us
    psum x1, waiting for transfers between devices, per_device(): query_grad = lax.psum(q_grad, 'entity')  69.5 us
    psum x1, waiting for transfers between devices, per_device(): lax.psum(teacher_part.astype(jnp.bfloat16), 'entity').astype(jnp.float32)  43.3 us
    dot_general x4, matrix products, first_pass(): t = jnp.dot(query_teacher, items[0].T, preferred_element_type=jnp.float32)  20.3 us
    unnamed x21, local copies, waits for them, and re-layouts  16.4 us
  transfers between devices with their start and end apart: 5, of which 5 were waited for; matrix products, arithmetic and copies ran while one was open for 4% of the time, Pallas kernels for 0%

commit v1 on v0

--- a/solution.py
+++ b/solution.py
@@ -37,7 +37,9 @@
     teacher_part = jnp.where(inside, jnp.take(teacher_slab, safe, axis=0).astype(jnp.float32), 0.0)
     student_part = jnp.where(inside, jnp.take(student_slab, safe, axis=0).astype(jnp.float32), 0.0)
     teacher_anchor, student_anchor = (
-        lax.psum(teacher_part.astype(jnp.bfloat16), "entity").astype(jnp.float32),
+        jnp.sum(lax.all_gather(teacher_part.astype(jnp.bfloat16), "entity"), axis=0).astype(
+            jnp.float32
+        ),
         lax.psum(student_part.astype(jnp.bfloat16), "entity").astype(jnp.float32),
     )
     query_teacher = query_vectors(

time: 745 us -> 834 us (1.12)
  waiting for transfers between devices: 581 us -> 659 us
    all_gather x0 -> x1, waiting for transfers between devices: none -> 89.3 us  [per_device(): lax.all_gather(teacher_part.astype(jnp.bfloat16), 'entity')]
    psum x1, waiting for transfers between devices: 43.3 us -> 31.5 us  [per_device(): lax.psum(student_part.astype(jnp.bfloat16), 'entity').astype(jnp.float32)]
  transfers between devices with their start and end apart: 5 -> 6, of which waited for: 5 -> 6; matrix products, arithmetic and copies ran while one was open for 4% -> 5% of each run, Pallas kernels for 0% -> 0%
where the time goes in v1:
time: 834 us; the launch traced here: 833 us
  waiting for transfers between devices  659 us (79%)
  matrix products  54 us (6%)
  local copies, waits for them, and re-layouts  40.8 us (5%)
  other arithmetic  34.7 us (4%)
  blocking collectives  29.1 us (3%)
  between operations  14.3 us (2%)
    reduce_scatter x1, waiting for transfers between devices, per_device(): lax.psum_scatter(slab_grad, 'query', scatter_dimension=0, tiled=True)  233 us
    all_gather x1, waiting for transfers between devices, per_device(): lax.all_gather(teacher_entities, 'query', axis=0, tiled=True)  150 us
    all_gather x1, waiting for transfers between devices, per_device(): lax.all_gather(teacher_part.astype(jnp.bfloat16), 'entity')  89.3 us
    all_gather x1, waiting for transfers between devices, per_device(): lax.all_gather(student_entities, 'query', axis=0, tiled=True)  83.7 us
    psum x1, waiting for transfers between devices, per_device(): query_grad = lax.psum(q_grad, 'entity')  70.9 us
    psum x1, waiting for transfers between devices, per_device(): lax.psum(student_part.astype(jnp.bfloat16), 'entity').astype(jnp.float32)  31.5 us
    dot_general x4, matrix products, first_pass(): t = jnp.dot(query_teacher, items[0].T, preferred_element_type=jnp.float32)  20.2 us
  transfers between devices with their start and end apart: 6, of which 6 were waited for; matrix products, arithmetic and copies ran while one was open for 5% of the time, Pallas kernels for 0%

profile of v1, /device:TPU:32, one launch (start us, length us, event | category | flops | bytes accessed | tf_op | source)
XLA Modules:
  0.0 833.1 jit_solution(13549640939313955465)
XLA Ops:
  8.0 1.8 copy.19
  10.6 83.7 %all-gather.8.cloned.1.call-done = bf16[4096,128]{1,0:T(8,128)(2,1)} async-done(((bf16[128,128]{1,0:T(8,128)(2,1)}), bf16[4096,128]{1,0:T(8,128)(2,1)}) %all-gather.8.cloned.1.call-update) | async-done | bytes 1048592 | tf_op jit(solution)/shard_map/all_gather | solution.py:30
  94.3 2.4 gather_fusion.2
  97.6 149.8 %all-gather.4.cloned.1.call-done = bf16[4096,1000]{1,0:T(8,128)(2,1)} async-done(((bf16[128,1000]{1,0:T(8,128)(2,1)}), bf16[4096,1000]{1,0:T(8,128)(2,1)}) %all-gather.4.cloned.1.call-update) | async-done | bytes 8192016 | tf_op jit(solution)/shard_map/all_gather | solution.py:29
  247.4 7.2 gather_fusion
  255.2 1.3 select_convert_fusion
  256.8 12.2 %copy.22 = bf16[4131,1000]{1,0:T(8,128)(2,1)} copy(bf16[4131,1000]{0,1:T(8,128)(2,1)} %param.16) | data formatting | bytes 16524000 | tf_op args[5]
  269.1 8.0 gather_fusion.1
  277.1 1.3 gather_fusion.3
  279.9 1.4 select_convert_fusion.1
  281.3 31.5 %all-reduce.5.cloned.1.call-done = bf16[512,128]{1,0:T(8,128)(2,1)} async-done(((bf16[512,128]{1,0:T(8,128)(2,1)}), bf16[512,128]{1,0:T(8,128)(2,1)}) %all-reduce.5.cloned.1.call-update) | async-done | bytes 131088 | tf_op jit(solution)/shard_map/psum | solution.py:43
  313.8 1.3 subtract_convert_fusion.2
  315.2 89.3 %all-gather.6.cloned.1.call-done = bf16[8,512,1000]{1,2,0:T(8,128)(2,1)} async-done(((bf16[1,512,1000]{1,2,0:T(8,128)(2,1)}), bf16[8,512,1000]{1,2,0:T(8,128)(2,1)}) %all-gather.6.cloned.1.call-update) | async-done | bytes 8192016 | tf_op jit(solution)/shard_map/all_gather | solution.py:40
  404.5 5.8 reduce_sum.39
  410.3 2.3 copy.21
  412.5 1.5 convert_element_type.49
  415.0 1.3 pad_maximum_fusion
  416.3 46.1 %while.32 = (s32[]{:T(128)}, f32[512]{0:T(512)S(1)}, f32[512]{0:T(512)}, f32[512]{0:T(512)}, f32[512]{0:T(512)}, /*index=5*/f32[512]{0:T(512)}, bf16[4,1024,1000...) while((s32[]{:T(128)}, f32[512]{0:T(512)S(1)}, ...), condition=%wide.region_8.9_spmd.clone, body=%wide.region_2.8_spmd.clone.sunk | while | flops 1187518464 | bytes 12046677 | solution.py:77
  416.3 5.1 fusion.51
  421.4 2.0 fusion.52
  424.8 2.4 multiply_reduce_fusion.2
  427.9 5.1 fusion.51
  432.9 2.0 fusion.52
  436.3 2.4 multiply_reduce_fusion.2
  439.4 5.1 fusion.51
  444.5 2.0 fusion.52
  447.8 2.4 multiply_reduce_fusion.2
  450.9 5.1 fusion.51
  456.0 2.0 fusion.52
  459.4 2.4 multiply_reduce_fusion.2
  462.5 14.5 %all-reduce.1 = (f32[512]{0:T(512)}, f32[512]{0:T(512)}) all-reduce(f32[512]{0:T(512)} %get-tuple-element.120, f32[512]{0:T(512)S(1)} %get-tuple-element.118), channel_id=1, replica_groups=mesh['query'=32,'entity'=8] {'entity'}, use_global_device_ids=true, to_apply=%region_12.13 | all-reduce | flops 1024 | bytes 8192 | tf_op jit(solution)/shard_map/pmax | solution.py:81
  477.7 14.7 %all-reduce = (f32[512]{0:T(512)S(1)}, f32[512]{0:T(512)}, f32[512]{0:T(512)}) all-reduce(f32[512]{0:T(512)S(1)} %get-tuple-element.259, f32[512]{0:T(512)S(1)} %get-tuple-element.257, f32[512]{0:T(512)S(1)} %get-tuple-element.256), channel_id=1, replica_groups=mesh['query'=32,'entity'=8] {'entity'}, use_global_device_ids=true, to_apply=%region_13.14 | all-reduce | flops 1536 | bytes 12288 | tf_op jit(solution)/shard_map/psum | solution.py:84
  492.3 26.0 %while.33 = (s32[]{:T(128)}, f32[512,128]{1,0:T(8,128)S(1)}, f32[4,1024,128]{2,1,0:T(8,128)}, bf16[4,1024,128]{2,1,0:T(8,128)(2,1)}, bf16[512,128]{1,0:T(8,128)(...) while((s32[]{:T(128)}, f32[512,128]{1,0:T(8,128)S(1)}, ...), condition=%wide.region_15.16_spmd.clone, body=%wide.region_14.15_spmd.clone.sunk | while | flops 1454505984 | bytes 16531671 | solution.py:101
  492.3 3.2 fusion.62
  495.6 1.5 subtract_convert_fusion.4
  497.6 1.3 fusion.63
  498.9 3.2 fusion.62
  502.1 1.5 subtract_convert_fusion.4
  504.1 1.3 fusion.63
  505.4 3.2 fusion.62
  508.7 1.5 subtract_convert_fusion.4
  510.7 1.2 fusion.63
  511.9 3.2 fusion.62
  515.2 1.5 subtract_convert_fusion.4
  519.7 1.3 log_add_fusion
  521.0 70.9 %all-reduce.7.cloned.1.call-done = f32[512,128]{1,0:T(8,128)} async-done(((f32[512,128]{1,0:T(8,128)}), f32[512,128]{1,0:T(8,128)}) %all-reduce.7.cloned.1.call-update) | async-done | bytes 262160 | tf_op jit(solution)/shard_map/psum | solution.py:104
  591.9 232.7 %reduce-scatter.2.cloned.1.call-done = f32[128,128]{1,0:T(8,128)} async-done(((f32[4096,128]{1,0:T(8,128)}), f32[128,128]{1,0:T(8,128)}) %reduce-scatter.2.cloned.1.call-update) | async-done | bytes 65552 | tf_op jit(solution)/shard_map/reduce_scatter | solution.py:103
  824.6 1.7 copy.53
  (145 shorter events, 20.1 us)
Async XLA Ops:
  7.2 269.9 %copy-start = (bf16[4131,128]{1,0:T(8,128)(2,1)S(1)}, bf16[4131,128]{1,0:T(8,128)(2,1)}, u32[]{:S(2)}) copy-start(bf16[4131,128]{1,0:T(8,128)(2,1)} %param.17) | copy-start | bytes 3172612
  7.2 87.1 %all-gather.8.cloned.1.call-start = ((), (), s32[]{:S(2)}) async-start(), calls=%async_computation.3 | async-start | bytes 1081344 | tf_op jit(solution)/shard_map/all_gather | solution.py:30
  7.9 239.5 %all-gather.4.cloned.1.call-start = ((), (), s32[]{:S(2)}) async-start(), calls=%async_computation.1 | async-start | bytes 8650752 | tf_op jit(solution)/shard_map/all_gather | solution.py:29
  9.8 303.0 %all-reduce.5.cloned.1.call-start = ((), (), s32[]{:S(2)}) async-start(), calls=%async_computation.4 | async-start | bytes 262144 | tf_op jit(solution)/shard_map/psum | solution.py:43
  97.6 307.0 %all-gather.6.cloned.1.call-start = ((), (), s32[]{:S(2)}) async-start(), calls=%async_computation.2 | async-start | bytes 9216000 | tf_op jit(solution)/shard_map/all_gather | solution.py:40
  256.5 335.4 %all-reduce.7.cloned.1.call-start = ((), (), s32[]{:S(2)}) async-start(), calls=%async_computation.6 | async-start | bytes 524288 | tf_op jit(solution)/shard_map/psum | solution.py:104
  256.8 12.3 %copy-start.12 = (s32[512]{0:T(512)S(1)}, s32[512]{0:T(512)}, u32[]{:S(2)}) copy-start(s32[512]{0:T(512)} %param.12) | copy-start | bytes 6148
  269.0 9.4 %copy-start.13 = (s32[512]{0:T(512)S(1)}, s32[512]{0:T(512)}, u32[]{:S(2)}) copy-start(s32[512]{0:T(512)} %param.13) | copy-start | bytes 6148
  279.9 33.9 %copy-start.10 = (f32[512]{0:T(512)S(1)}, f32[512]{0:T(512)}, u32[]{:S(2)}) copy-start(f32[512]{0:T(512)} %add_convert_fusion.2) | copy-start | bytes 6148
  412.5 1.5 copy-start.11
  424.8 2.4 copy-start.3
  424.8 2.4 copy-start.4
  424.8 2.4 copy-start.6
  424.8 2.4 copy-start.8
  427.2 0.6 copy-start.5
  427.2 0.6 copy-start.7
  427.2 0.6 copy-start.9
  436.3 2.4 copy-start.3
  436.3 2.4 copy-start.4
  436.3 2.4 copy-start.6
  436.3 2.4 copy-start.8
  438.7 0.6 copy-start.5
  438.8 0.6 copy-start.7
  447.8 2.4 copy-start.3
  447.8 2.4 copy-start.4
  447.8 2.4 copy-start.6
  447.8 2.4 copy-start.8
  450.3 0.6 copy-start.5
  450.3 0.6 copy-start.7
  450.3 0.6 copy-start.9
  459.4 2.4 copy-start.3
  459.4 2.4 copy-start.4
  459.4 2.4 copy-start.6
  459.4 2.4 copy-start.8
  461.8 0.6 copy-start.5
  461.8 0.6 copy-start.7
  492.3 3.2 copy-start.1
  492.3 3.2 copy-start.14
  498.9 3.2 copy-start.1
  498.9 3.2 copy-start.14
  505.4 3.2 copy-start.1
  505.4 3.2 copy-start.14
  511.9 3.2 copy-start.1
  511.9 3.2 copy-start.14
  518.4 0.7 copy-start.2
  518.4 1.3 copy-start.15
  518.4 1.3 copy-start.16
  519.1 305.5 %reduce-scatter.2.cloned.1.call-start = ((), (), s32[]{:S(2)}) async-start(), calls=%async_computation.5 | async-start | bytes 2162688 | tf_op jit(solution)/shard_map/reduce_scatter | solution.py:103
  (2 other events, 1.3 us)
Sparse Core Ops, SparseCore 0:
  11.4 82.7 all-gather.7
  98.4 149.0 all-gather.3
  250.1 62.7 all-reduce.4
  314.6 89.8 all-gather.5
  519.2 72.6 all-reduce.6
  594.8 229.7 reduce-scatter.1
